TPU v7x, 512 devices: a whole 4x8x8 slice. The times are simulated.
512 devices in a mesh: src: 8 (over x, y_lo), gx: 16 (over z, core), gy: 4 (over y_hi).
Axes of the slice: x: 4, y: 8 (y_hi: 4, y_lo: 2; y = y_hi * 2 + y_lo), z: 8, core: 2. Of those that a mesh axis runs over, the one named last changes fastest.
Arguments:
- warm_potential: float32 [32, 64, 128, 128], P('src', 'gx', 'gy'), may hold values from -3 to 3
- warm_adjoint: float32 [32, 64, 128, 128], P('src', 'gx', 'gy'), may hold values from -3 to 3
- conductivity: float32 [64, 128, 128], P('gx', 'gy', 'src'), may hold values from 0.2 to 5
- electrodes: int32 [32, 2], replicated, may hold values from 0 to 8191
- receivers: int32 [128, 2], replicated, may hold values from 0 to 8191
- observed: float32 [32, 128], replicated, may hold values from -6 to 6
- source_order: int32 [32], replicated, may hold values from 0 to 31, each once
Outputs:
- gradient: float32 [64, 128, 128], P('gx', 'gy', 'src')
Inputs may be any that keep to these rules, and one draw needn't show every extreme that they name: `electrodes`: entries number surface cells as x * 128 + y. `receivers`: entries number surface cells as x * 128 + y.
All inputs are finite; a program needn't handle non-finite values.
Results may differ from a plain program's by a relative error of at most 0.0003.
Values sent between devices are 32-bit elements; how exact they have to be, the bound alone decides.
A program may use at most 64 MiB of HBM per device.

v0:
```python
import jax
import jax.numpy as jnp
from jax import lax
from jax.sharding import PartitionSpec as P

SWEEPS = 6
lowest = 0.05
highest = 2.0
centre = (highest + lowest) / 2.0
half_span = (highest - lowest) / 2.0
bound_ratio = centre / half_span
strength = 4.0


def padded_2(block, sides, width):
    for axis, dim in sides:
        count = lax.axis_size(axis)
        forward = [(i, i + 1) for i in range(count - 1)]
        backward = [(target, source) for source, target in forward]
        low = lax.ppermute(
            lax.slice_in_dim(block, block.shape[dim] - width, None, axis=dim), axis, forward
        )
        high = lax.ppermute(lax.slice_in_dim(block, 0, width, axis=dim), axis, backward)
        block = jnp.concatenate([low, block, high], axis=dim)
    return block


def harmonic(left, right):
    return jnp.where(right > 0, 2.0 * left * right / (left + right), left)


def slope_of(left, right):
    total = left + right
    return jnp.where(right > 0, 2.0 * right * right / (total * total), 1.0)


def neighbours(field, padded):
    widths = [(0, 0)] * (field.ndim - 1) + [(1, 1)]
    deeper = jnp.pad(field, widths)
    return (
        padded[..., :-2, 1:-1, :],
        padded[..., 2:, 1:-1, :],
        padded[..., 1:-1, :-2, :],
        padded[..., 1:-1, 2:, :],
        deeper[..., :-2],
        deeper[..., 2:],
    )


def face_tables(sigma, padded):
    others = neighbours(sigma, padded)
    depth = lax.broadcasted_iota(jnp.int32, sigma.shape, 2)
    surface = depth == 0
    coeffs = [harmonic(sigma, other) for other in others]
    slopes = [slope_of(sigma, other) for other in others]
    coeffs[4] = jnp.where(surface, 0.0, coeffs[4])
    slopes[4] = jnp.where(surface, 0.0, slopes[4])
    return (coeffs, slopes)


def apply_operator(field, padded, coeffs):
    others = neighbours(field, padded)
    total = coeffs[0] * (field - others[0])
    for index in range(1, 6):
        total = total + coeffs[index] * (field - others[index])
    return total


def solve(rhs, start, coeffs, inverse, pad_fn):
    residual = rhs - apply_operator(start, pad_fn(start), coeffs)
    update = inverse * residual / centre
    iterate = start
    factor = 1.0 / bound_ratio
    for sweep in range(SWEEPS):
        iterate = iterate + update
        residual = residual - apply_operator(update, pad_fn(update), coeffs)
        following = 1.0 / (2.0 * bound_ratio - factor)
        update = following * factor * update + 2.0 * following / half_span * (inverse * residual)
        factor = following
    return iterate + update


def gradient_term(potential, adjoint, padded_potential, padded_adjoint, slopes):
    near_potential = neighbours(potential, padded_potential)
    near_adjoint = neighbours(adjoint, padded_adjoint)
    total = slopes[0] * (potential - near_potential[0]) * (adjoint - near_adjoint[0])
    for index in range(1, 6):
        total = total + slopes[index] * (potential - near_potential[index]) * (
            adjoint - near_adjoint[index]
        )
    return total


def pad_joint(field):
    return padded_2(field, (("gx", 1), ("gy", 2)), 1)


def reduce_groups(partial_value, depth):
    summed = lax.psum(partial_value, "src")
    return lax.dynamic_slice_in_dim(summed, lax.axis_index("src") * depth, depth, 2)


def body(warm_potential, warm_adjoint, conductivity, electrodes, receivers, observed, source_order):
    panel = lax.all_gather(conductivity, "src", axis=2, tiled=True)
    group = lax.axis_index("src")
    slots = warm_potential.shape[0]
    width_x = panel.shape[0]
    ny_global = panel.shape[1] * lax.axis_size("gy")
    x_start = lax.axis_index("gx") * width_x
    potential_start, adjoint_start = (warm_potential, warm_adjoint)
    first_slot = group * slots
    y_start = lax.axis_index("gy") * panel.shape[1]
    width_y = panel.shape[1]
    depth_cells = panel.shape[2]
    coeffs, slopes = face_tables(panel, pad_joint(panel[None])[0])
    inverse = 1.0 / (coeffs[0] + coeffs[1] + coeffs[2] + coeffs[3] + coeffs[4] + coeffs[5])
    idents = lax.dynamic_slice_in_dim(source_order, first_slot, slots)
    pairs = jnp.take(electrodes, idents, axis=0)
    rows_observed = jnp.take(observed, idents, axis=0)

    def picker(cells):
        local_x = cells // ny_global - x_start
        local_y = cells % ny_global - y_start
        inside = (local_x >= 0) & (local_x < width_x) & (local_y >= 0) & (local_y < width_y)
        flat = local_x * width_y + local_y
        places = lax.broadcasted_iota(jnp.int32, (cells.shape[0], width_x * width_y), 1)
        return jnp.where((flat[:, None] == places) & inside[:, None], 1.0, 0.0).astype(jnp.float32)

    def on_surface(flat):
        field = jnp.zeros((slots, width_x, width_y, depth_cells), jnp.float32)
        return field.at[..., 0].set(flat.reshape(slots, width_x, width_y))

    source_surface = strength * (picker(pairs[:, 0]) - picker(pairs[:, 1]))
    potential = solve(on_surface(source_surface), potential_start, coeffs, inverse, pad_joint)
    pickup = picker(receivers[:, 0]) - picker(receivers[:, 1])
    top = potential[..., 0].reshape(slots, width_x * width_y)
    local_values = jnp.dot(
        top, pickup.T, precision=lax.Precision.HIGHEST, preferred_element_type=jnp.float32
    )
    predicted = lax.psum(local_values, ("gx", "gy"))
    misfit = predicted - rows_observed
    back = jnp.dot(
        misfit, pickup, precision=lax.Precision.HIGHEST, preferred_element_type=jnp.float32
    )
    adjoint = solve(on_surface(back), adjoint_start, coeffs, inverse, pad_joint)
    padded_both = pad_joint(jnp.concatenate([potential, adjoint], 0))
    term = gradient_term(potential, adjoint, padded_both[:slots], padded_both[slots:], slopes)
    partial_value = -jnp.sum(term, axis=0)
    return reduce_groups(partial_value, conductivity.shape[2])


def solution(mesh):
    in_specs = (
        P("src", "gx", "gy", None),
        P("src", "gx", "gy", None),
        P("gx", "gy", "src"),
        P(),
        P(),
        P(),
        P(),
    )
    out_specs = P("gx", "gy", "src")
    return jax.shard_map(body, mesh=mesh, in_specs=in_specs, out_specs=out_specs, check_vma=False)
```

profile of v0, /device:TPU:16, one launch (start us, length us, event | category | flops | bytes accessed | tf_op | source)
XLA Modules:
  0.0 592.4 jit_solution(16727907163246744626)
XLA Ops:
  7.3 29.0 %all_gather.3 = f32[4,32,128]{1,0,2:T(4,128)S(1)} all-gather(f32[4,32,16]{1,0,2:T(4,128)S(1)} %copy.69), channel_id=1, replica_groups=mesh['src'=8,'gx'=16,'gy'=4] {'src'}, dimensions={2}, use_global_device_ids=true | all-gather | bytes 73728 | tf_op jit(solution)/shard_map/all_gather | solution.py:104
  36.5 1.3 collective-permute-start.1
  37.8 3.0 collective-permute-start
  40.9 3.9 collective-permute-start.4
  50.0 5.4 collective-permute-start.3
  55.4 2.6 collective-permute-start.2
  58.0 21.9 %collective-permute-done.3 = f32[1,6,1,128]{2,1,3,0:T(8,128)S(1)} collective-permute-done((f32[1,6,1,128]{2,1,3,0:T(8,128)S(1)}, f32[1,6,1,128]{2,1,3,0:T(8,128)S(1)}, u32[]{:S(2)}, u32[]{:S(2)}) %collective-permute-start.3) | collective-permute-done | bytes 3104 | tf_op jit(solution)/shard_map/ppermute | solution.py:23
  80.5 1.7 fusion.293
  82.3 2.3 collective-permute-start.7
  84.7 5.6 collective-permute-start.6
  90.3 2.0 add_divide_fusion
  96.5 3.0 collective-permute-start.8
  100.5 1.9 collective-permute-start.11
  102.4 6.0 %collective-permute-start.10 = (f32[4,6,1,128]{3,2,1,0:T(1,128)S(1)}, f32[4,6,1,128]{3,2,1,0:T(1,128)S(1)}, u32[]{:S(2)}, u32[]{:S(2)}) collective-permute-start(f32[4,6,1,128]{3,2,1,0:T(1,128)S(1)} %get-tuple-element.118), channel_id=1, source_target_pairs={{0,1},{1,2},{2,3},{4,5},{5,6},{6,7},{8,9},{9,10},{10,11},{12,13},{... | collective-permute-start | bytes 36872 | tf_op jit(solution)/shard_map/ppermute | solution.py:20
  108.5 1.4 collective-permute-done.10
  111.4 5.8 collective-permute-start.12
  118.2 1.9 collective-permute-start.15
  120.1 6.0 %collective-permute-start.14 = (f32[4,6,1,128]{3,2,1,0:T(1,128)S(1)}, f32[4,6,1,128]{3,2,1,0:T(1,128)S(1)}, u32[]{:S(2)}, u32[]{:S(2)}) collective-permute-start(f32[4,6,1,128]{3,2,1,0:T(1,128)S(1)} %get-tuple-element.116), channel_id=1, source_target_pairs={{0,1},{1,2},{2,3},{4,5},{5,6},{6,7},{8,9},{9,10},{10,11},{12,13},{... | collective-permute-start | bytes 36872 | tf_op jit(solution)/shard_map/ppermute | solution.py:20
  126.2 1.4 collective-permute-done.14
  127.8 1.4 collective-permute-start.17
  129.3 5.9 collective-permute-start.16
  136.1 1.9 collective-permute-start.19
  138.0 6.0 %collective-permute-start.18 = (f32[4,6,1,128]{3,2,1,0:T(1,128)S(1)}, f32[4,6,1,128]{3,2,1,0:T(1,128)S(1)}, u32[]{:S(2)}, u32[]{:S(2)}) collective-permute-start(f32[4,6,1,128]{3,2,1,0:T(1,128)S(1)} %get-tuple-element.114), channel_id=1, source_target_pairs={{0,1},{1,2},{2,3},{4,5},{5,6},{6,7},{8,9},{9,10},{10,11},{12,13},{... | collective-permute-start | bytes 36872 | tf_op jit(solution)/shard_map/ppermute | solution.py:20
  144.7 5.5 collective-permute-start.32
  153.2 5.8 collective-permute-start.20
  160.5 1.9 collective-permute-start.23
  162.4 6.0 %collective-permute-start.22 = (f32[4,6,1,128]{3,2,1,0:T(1,128)}, f32[4,6,1,128]{3,2,1,0:T(1,128)}, u32[]{:S(2)}, u32[]{:S(2)}) collective-permute-start(f32[4,6,1,128]{3,2,1,0:T(1,128)} %get-tuple-element.112), channel_id=1, source_target_pairs={{0,1},{1,2},{2,3},{4,5},{5,6},{6,7},{8,9},{9,10},{10,11},{12,13},{... | collective-permute-start | bytes 36872 | tf_op jit(solution)/shard_map/ppermute | solution.py:20
  172.6 4.1 collective-permute-start.24
  177.6 1.9 collective-permute-start.27
  179.5 6.0 %collective-permute-start.26 = (f32[4,6,1,128]{3,2,1,0:T(1,128)S(1)}, f32[4,6,1,128]{3,2,1,0:T(1,128)S(1)}, u32[]{:S(2)}, u32[]{:S(2)}) collective-permute-start(f32[4,6,1,128]{3,2,1,0:T(1,128)S(1)} %get-tuple-element.110), channel_id=1, source_target_pairs={{0,1},{1,2},{2,3},{4,5},{5,6},{6,7},{8,9},{9,10},{10,11},{12,13},{... | collective-permute-start | bytes 36872 | tf_op jit(solution)/shard_map/ppermute | solution.py:20
  185.6 1.3 collective-permute-done.26
  188.6 5.2 collective-permute-start.28
  194.7 1.9 collective-permute-start.31
  196.6 6.0 %collective-permute-start.30 = (f32[4,6,1,128]{3,2,1,0:T(1,128)S(1)}, f32[4,6,1,128]{3,2,1,0:T(1,128)S(1)}, u32[]{:S(2)}, u32[]{:S(2)}) collective-permute-start(f32[4,6,1,128]{3,2,1,0:T(1,128)S(1)} %get-tuple-element.108), channel_id=1, source_target_pairs={{0,1},{1,2},{2,3},{4,5},{5,6},{6,7},{8,9},{9,10},{10,11},{12,13},{... | collective-permute-start | bytes 36872 | tf_op jit(solution)/shard_map/ppermute | solution.py:20
  202.7 1.9 collective-permute-start.35
  204.6 6.0 %collective-permute-start.34 = (f32[4,6,1,128]{3,2,1,0:T(1,128)S(1)}, f32[4,6,1,128]{3,2,1,0:T(1,128)S(1)}, u32[]{:S(2)}, u32[]{:S(2)}) collective-permute-start(f32[4,6,1,128]{3,2,1,0:T(1,128)S(1)} %get-tuple-element.106), channel_id=1, source_target_pairs={{0,1},{1,2},{2,3},{4,5},{5,6},{6,7},{8,9},{9,10},{10,11},{12,13},{... | collective-permute-start | bytes 36872 | tf_op jit(solution)/shard_map/ppermute | solution.py:20
  212.4 144.6 %psum.14 = f32[4,128]{1,0:T(4,128)S(1)} all-reduce(f32[4,128]{1,0:T(4,128)S(1)} %fusion.300), channel_id=1, replica_groups=mesh['src'=8,'gx'=16,'gy'=4] {'gx','gy'}, use_global_device_ids=true, to_apply=%region_0.1 | all-reduce | flops 512 | bytes 4096 | tf_op jit(solution)/shard_map/psum | solution.py:140
  359.9 3.0 collective-permute-start.36
  363.9 4.6 collective-permute-start.39
  368.5 3.3 collective-permute-start.38
  371.9 3.1 collective-permute-done.38
  376.6 3.0 collective-permute-start.40
  380.6 1.9 collective-permute-start.43
  382.5 6.0 %collective-permute-start.42 = (f32[4,6,1,128]{3,2,1,0:T(1,128)S(1)}, f32[4,6,1,128]{3,2,1,0:T(1,128)S(1)}, u32[]{:S(2)}, u32[]{:S(2)}) collective-permute-start(f32[4,6,1,128]{3,2,1,0:T(1,128)S(1)} %get-tuple-element.102), channel_id=1, source_target_pairs={{0,1},{1,2},{2,3},{4,5},{5,6},{6,7},{8,9},{9,10},{10,11},{12,13},{... | collective-permute-start | bytes 36872 | tf_op jit(solution)/shard_map/ppermute | solution.py:20
  388.5 1.4 collective-permute-done.42
  391.5 4.1 collective-permute-start.44
  396.6 1.9 collective-permute-start.47
  398.5 6.2 %collective-permute-start.46 = (f32[4,6,1,128]{3,2,1,0:T(1,128)S(1)}, f32[4,6,1,128]{3,2,1,0:T(1,128)S(1)}, u32[]{:S(2)}, u32[]{:S(2)}) collective-permute-start(f32[4,6,1,128]{3,2,1,0:T(1,128)S(1)} %get-tuple-element.100), channel_id=1, source_target_pairs={{0,1},{1,2},{2,3},{4,5},{5,6},{6,7},{8,9},{9,10},{10,11},{12,13},{... | collective-permute-start | bytes 36872 | tf_op jit(solution)/shard_map/ppermute | solution.py:20
  407.5 5.9 collective-permute-start.48
  414.3 1.9 collective-permute-start.51
  416.3 6.0 %collective-permute-start.50 = (f32[4,6,1,128]{3,2,1,0:T(1,128)S(1)}, f32[4,6,1,128]{3,2,1,0:T(1,128)S(1)}, u32[]{:S(2)}, u32[]{:S(2)}) collective-permute-start(f32[4,6,1,128]{3,2,1,0:T(1,128)S(1)} %get-tuple-element.98), channel_id=1, source_target_pairs={{0,1},{1,2},{2,3},{4,5},{5,6},{6,7},{8,9},{9,10},{10,11},{12,13},{... | collective-permute-start | bytes 36872 | tf_op jit(solution)/shard_map/ppermute | solution.py:20
  422.3 1.4 collective-permute-done.50
  425.3 5.6 collective-permute-start.52
  431.8 1.9 collective-permute-start.55
  433.7 6.0 %collective-permute-start.54 = (f32[4,6,1,128]{3,2,1,0:T(1,128)S(1)}, f32[4,6,1,128]{3,2,1,0:T(1,128)S(1)}, u32[]{:S(2)}, u32[]{:S(2)}) collective-permute-start(f32[4,6,1,128]{3,2,1,0:T(1,128)S(1)} %get-tuple-element.96), channel_id=1, source_target_pairs={{0,1},{1,2},{2,3},{4,5},{5,6},{6,7},{8,9},{9,10},{10,11},{12,13},{... | collective-permute-start | bytes 36872 | tf_op jit(solution)/shard_map/ppermute | solution.py:20
  439.8 1.4 collective-permute-done.54
  442.8 5.6 collective-permute-start.56
  449.3 1.9 collective-permute-start.59
  451.2 6.0 %collective-permute-start.58 = (f32[4,6,1,128]{3,2,1,0:T(1,128)S(1)}, f32[4,6,1,128]{3,2,1,0:T(1,128)S(1)}, u32[]{:S(2)}, u32[]{:S(2)}) collective-permute-start(f32[4,6,1,128]{3,2,1,0:T(1,128)S(1)} %get-tuple-element.94), channel_id=1, source_target_pairs={{0,1},{1,2},{2,3},{4,5},{5,6},{6,7},{8,9},{9,10},{10,11},{12,13},{... | collective-permute-start | bytes 36872 | tf_op jit(solution)/shard_map/ppermute | solution.py:20
  457.3 1.4 collective-permute-done.58
  460.4 5.7 collective-permute-start.60
  467.2 2.1 collective-permute-start.63
  469.2 6.0 %collective-permute-start.62 = (f32[8,6,1,128]{3,2,1,0:T(1,128)S(1)}, f32[8,6,1,128]{3,2,1,0:T(1,128)S(1)}, u32[]{:S(2)}, u32[]{:S(2)}) collective-permute-start(f32[8,6,1,128]{3,2,1,0:T(1,128)S(1)} %get-tuple-element.82), channel_id=1, source_target_pairs={{0,1},{1,2},{2,3},{4,5},{5,6},{6,7},{8,9},{9,10},{10,11},{12,13},{... | collective-permute-start | bytes 73736 | tf_op jit(solution)/shard_map/ppermute | solution.py:20
  477.8 106.1 %all-reduce.21.cloned.1.call-done = f32[4,32,128]{2,1,0:T(8,128)} async-done(((f32[4,32,128]{2,1,0:T(8,128)}), f32[4,32,128]{2,1,0:T(8,128)}) %all-reduce.21.cloned.1.call-update) | async-done | bytes 65552 | tf_op jit(solution)/shard_map/psum | solution.py:99
  (203 shorter events, 54.0 us)
Async XLA Ops:
  6.5 577.4 %all-reduce.21.cloned.1.call-start = ((), (), s32[]{:S(2)}) async-start(), calls=%async_computation | async-start | bytes 131072 | tf_op jit(solution)/shard_map/psum | solution.py:99
  36.5 13.1 %collective-permute-start.1 = (f32[1,1,32,128]{2,1,3,0:T(1,128)S(1)}, f32[1,1,32,128]{2,1,3,0:T(1,128)S(1)}, u32[]{:S(2)}, u32[]{:S(2)}) collective-permute-start(f32[1,1,32,128]{2,1,3,0:T(1,128)S(1)} %get-tuple-element.153), channel_id=1, source_target_pairs={{4,0},{8,4},{12,8},{16,12},{20,16},{24,20},{28,24},{32,28},{36,32}... | collective-permute-start | bytes 49160 | tf_op jit(solution)/shard_map/ppermute | solution.py:23
  37.8 11.8 %collective-permute-start = (f32[1,1,32,128]{2,1,3,0:T(1,128)S(1)}, f32[1,1,32,128]{2,1,3,0:T(1,128)S(1)}, u32[]{:S(2)}, u32[]{:S(2)}) collective-permute-start(f32[1,1,32,128]{2,1,3,0:T(1,128)S(1)} %get-tuple-element.152), channel_id=1, source_target_pairs={{0,4},{4,8},{8,12},{12,16},{16,20},{20,24},{24,28},{28,32},{32,36}... | collective-permute-start | bytes 49160 | tf_op jit(solution)/shard_map/ppermute | solution.py:20
  40.9 41.4 %collective-permute-start.4 = (f32[4,1,32,128]{3,2,1,0:T(8,128)S(1)}, f32[4,1,32,128]{3,2,1,0:T(8,128)S(1)}, u32[]{:S(2)}, u32[]{:S(2)}) collective-permute-start(f32[4,1,32,128]{3,2,1,0:T(8,128)S(1)} %get-tuple-element.151), channel_id=1, source_target_pairs={{0,4},{4,8},{8,12},{12,16},{16,20},{20,24},{24,28},{28,32},{32,36}... | collective-permute-start | bytes 196616 | tf_op jit(solution)/shard_map/ppermute | solution.py:20
  44.8 37.5 %collective-permute-start.5 = (f32[4,1,32,128]{3,2,1,0:T(8,128)S(1)}, f32[4,1,32,128]{3,2,1,0:T(8,128)S(1)}, u32[]{:S(2)}, u32[]{:S(2)}) collective-permute-start(f32[4,1,32,128]{3,2,1,0:T(8,128)S(1)} %get-tuple-element.150), channel_id=1, source_target_pairs={{4,0},{8,4},{12,8},{16,12},{20,16},{24,20},{28,24},{32,28},{36,32}... | collective-permute-start | bytes 196616 | tf_op jit(solution)/shard_map/ppermute | solution.py:23
  50.0 29.9 %collective-permute-start.3 = (f32[1,6,1,128]{2,1,3,0:T(8,128)S(1)}, f32[1,6,1,128]{2,1,3,0:T(8,128)S(1)}, u32[]{:S(2)}, u32[]{:S(2)}) collective-permute-start(f32[1,6,1,128]{2,1,3,0:T(8,128)S(1)} %get-tuple-element.93), channel_id=1, source_target_pairs={{1,0},{2,1},{3,2},{5,4},{6,5},{7,6},{9,8},{10,9},{11,10},{13,12},{... | collective-permute-start | bytes 9224 | tf_op jit(solution)/shard_map/ppermute | solution.py:23
  55.4 24.5 %collective-permute-start.2 = (f32[1,6,1,128]{2,1,3,0:T(8,128)S(1)}, f32[1,6,1,128]{2,1,3,0:T(8,128)S(1)}, u32[]{:S(2)}, u32[]{:S(2)}) collective-permute-start(f32[1,6,1,128]{2,1,3,0:T(8,128)S(1)} %get-tuple-element.92), channel_id=1, source_target_pairs={{0,1},{1,2},{2,3},{4,5},{5,6},{6,7},{8,9},{9,10},{10,11},{12,13},{... | collective-permute-start | bytes 9224 | tf_op jit(solution)/shard_map/ppermute | solution.py:20
  82.3 11.8 %collective-permute-start.7 = (f32[4,6,1,128]{3,2,1,0:T(1,128)S(1)}, f32[4,6,1,128]{3,2,1,0:T(1,128)S(1)}, u32[]{:S(2)}, u32[]{:S(2)}) collective-permute-start(f32[4,6,1,128]{3,2,1,0:T(1,128)S(1)} %get-tuple-element.121), channel_id=1, source_target_pairs={{1,0},{2,1},{3,2},{5,4},{6,5},{7,6},{9,8},{10,9},{11,10},{13,12},{... | collective-permute-start | bytes 36872 | tf_op jit(solution)/shard_map/ppermute | solution.py:23
  84.7 9.4 %collective-permute-start.6 = (f32[4,6,1,128]{3,2,1,0:T(1,128)S(1)}, f32[4,6,1,128]{3,2,1,0:T(1,128)S(1)}, u32[]{:S(2)}, u32[]{:S(2)}) collective-permute-start(f32[4,6,1,128]{3,2,1,0:T(1,128)S(1)} %get-tuple-element.120), channel_id=1, source_target_pairs={{0,1},{1,2},{2,3},{4,5},{5,6},{6,7},{8,9},{9,10},{10,11},{12,13},{... | collective-permute-start | bytes 36872 | tf_op jit(solution)/shard_map/ppermute | solution.py:20
  95.2 4.3 collective-permute-start.9
  96.5 3.9 collective-permute-start.8
  100.5 8.0 %collective-permute-start.11 = (f32[4,6,1,128]{3,2,1,0:T(1,128)S(1)}, f32[4,6,1,128]{3,2,1,0:T(1,128)S(1)}, u32[]{:S(2)}, u32[]{:S(2)}) collective-permute-start(f32[4,6,1,128]{3,2,1,0:T(1,128)S(1)} %get-tuple-element.119), channel_id=1, source_target_pairs={{1,0},{2,1},{3,2},{5,4},{6,5},{7,6},{9,8},{10,9},{11,10},{13,12},{... | collective-permute-start | bytes 36872 | tf_op jit(solution)/shard_map/ppermute | solution.py:23
  102.4 7.4 %collective-permute-start.10 = (f32[4,6,1,128]{3,2,1,0:T(1,128)S(1)}, f32[4,6,1,128]{3,2,1,0:T(1,128)S(1)}, u32[]{:S(2)}, u32[]{:S(2)}) collective-permute-start(f32[4,6,1,128]{3,2,1,0:T(1,128)S(1)} %get-tuple-element.118), channel_id=1, source_target_pairs={{0,1},{1,2},{2,3},{4,5},{5,6},{6,7},{8,9},{9,10},{10,11},{12,13},{... | collective-permute-start | bytes 36872 | tf_op jit(solution)/shard_map/ppermute | solution.py:20
  110.1 7.1 %collective-permute-start.13 = (f32[4,1,32,128]{3,2,1,0:T(8,128)S(1)}, f32[4,1,32,128]{3,2,1,0:T(8,128)S(1)}, u32[]{:S(2)}, u32[]{:S(2)}) collective-permute-start(f32[4,1,32,128]{3,2,1,0:T(8,128)S(1)} %get-tuple-element.147), channel_id=1, source_target_pairs={{4,0},{8,4},{12,8},{16,12},{20,16},{24,20},{28,24},{32,28},{36,32}... | collective-permute-start | bytes 196616 | tf_op jit(solution)/shard_map/ppermute | solution.py:23
  111.4 6.7 %collective-permute-start.12 = (f32[4,1,32,128]{3,2,1,0:T(8,128)S(1)}, f32[4,1,32,128]{3,2,1,0:T(8,128)S(1)}, u32[]{:S(2)}, u32[]{:S(2)}) collective-permute-start(f32[4,1,32,128]{3,2,1,0:T(8,128)S(1)} %get-tuple-element.146), channel_id=1, source_target_pairs={{0,4},{4,8},{8,12},{12,16},{16,20},{20,24},{24,28},{28,32},{32,36}... | collective-permute-start | bytes 196616 | tf_op jit(solution)/shard_map/ppermute | solution.py:20
  118.2 8.0 %collective-permute-start.15 = (f32[4,6,1,128]{3,2,1,0:T(1,128)S(1)}, f32[4,6,1,128]{3,2,1,0:T(1,128)S(1)}, u32[]{:S(2)}, u32[]{:S(2)}) collective-permute-start(f32[4,6,1,128]{3,2,1,0:T(1,128)S(1)} %get-tuple-element.117), channel_id=1, source_target_pairs={{1,0},{2,1},{3,2},{5,4},{6,5},{7,6},{9,8},{10,9},{11,10},{13,12},{... | collective-permute-start | bytes 36872 | tf_op jit(solution)/shard_map/ppermute | solution.py:23
  120.1 7.4 %collective-permute-start.14 = (f32[4,6,1,128]{3,2,1,0:T(1,128)S(1)}, f32[4,6,1,128]{3,2,1,0:T(1,128)S(1)}, u32[]{:S(2)}, u32[]{:S(2)}) collective-permute-start(f32[4,6,1,128]{3,2,1,0:T(1,128)S(1)} %get-tuple-element.116), channel_id=1, source_target_pairs={{0,1},{1,2},{2,3},{4,5},{5,6},{6,7},{8,9},{9,10},{10,11},{12,13},{... | collective-permute-start | bytes 36872 | tf_op jit(solution)/shard_map/ppermute | solution.py:20
  127.8 7.3 %collective-permute-start.17 = (f32[4,1,32,128]{3,2,1,0:T(8,128)S(1)}, f32[4,1,32,128]{3,2,1,0:T(8,128)S(1)}, u32[]{:S(2)}, u32[]{:S(2)}) collective-permute-start(f32[4,1,32,128]{3,2,1,0:T(8,128)S(1)} %get-tuple-element.145), channel_id=1, source_target_pairs={{4,0},{8,4},{12,8},{16,12},{20,16},{24,20},{28,24},{32,28},{36,32}... | collective-permute-start | bytes 196616 | tf_op jit(solution)/shard_map/ppermute | solution.py:23
  129.3 6.8 %collective-permute-start.16 = (f32[4,1,32,128]{3,2,1,0:T(8,128)S(1)}, f32[4,1,32,128]{3,2,1,0:T(8,128)S(1)}, u32[]{:S(2)}, u32[]{:S(2)}) collective-permute-start(f32[4,1,32,128]{3,2,1,0:T(8,128)S(1)} %get-tuple-element.144), channel_id=1, source_target_pairs={{0,4},{4,8},{8,12},{12,16},{16,20},{20,24},{24,28},{28,32},{32,36}... | collective-permute-start | bytes 196616 | tf_op jit(solution)/shard_map/ppermute | solution.py:20
  136.1 15.5 %collective-permute-start.19 = (f32[4,6,1,128]{3,2,1,0:T(1,128)S(1)}, f32[4,6,1,128]{3,2,1,0:T(1,128)S(1)}, u32[]{:S(2)}, u32[]{:S(2)}) collective-permute-start(f32[4,6,1,128]{3,2,1,0:T(1,128)S(1)} %get-tuple-element.115), channel_id=1, source_target_pairs={{1,0},{2,1},{3,2},{5,4},{6,5},{7,6},{9,8},{10,9},{11,10},{13,12},{... | collective-permute-start | bytes 36872 | tf_op jit(solution)/shard_map/ppermute | solution.py:23
  138.0 13.6 %collective-permute-start.18 = (f32[4,6,1,128]{3,2,1,0:T(1,128)S(1)}, f32[4,6,1,128]{3,2,1,0:T(1,128)S(1)}, u32[]{:S(2)}, u32[]{:S(2)}) collective-permute-start(f32[4,6,1,128]{3,2,1,0:T(1,128)S(1)} %get-tuple-element.114), channel_id=1, source_target_pairs={{0,1},{1,2},{2,3},{4,5},{5,6},{6,7},{8,9},{9,10},{10,11},{12,13},{... | collective-permute-start | bytes 36872 | tf_op jit(solution)/shard_map/ppermute | solution.py:20
  144.7 32.0 %collective-permute-start.32 = (f32[4,1,32,128]{3,2,1,0:T(8,128)}, f32[4,1,32,128]{3,2,1,0:T(8,128)S(1)}, u32[]{:S(2)}, u32[]{:S(2)}) collective-permute-start(f32[4,1,32,128]{3,2,1,0:T(8,128)} %get-tuple-element.137), channel_id=1, source_target_pairs={{0,4},{4,8},{8,12},{12,16},{16,20},{20,24},{24,28},{28,32},{32,36}... | collective-permute-start | bytes 196616 | tf_op jit(solution)/shard_map/ppermute | solution.py:20
  150.2 43.6 %collective-permute-start.33 = (f32[4,1,32,128]{3,2,1,0:T(8,128)}, f32[4,1,32,128]{3,2,1,0:T(8,128)}, u32[]{:S(2)}, u32[]{:S(2)}) collective-permute-start(f32[4,1,32,128]{3,2,1,0:T(8,128)} %get-tuple-element.136), channel_id=1, source_target_pairs={{4,0},{8,4},{12,8},{16,12},{20,16},{24,20},{28,24},{32,28},{36,32}... | collective-permute-start | bytes 196616 | tf_op jit(solution)/shard_map/ppermute | solution.py:23
  151.9 7.7 %collective-permute-start.21 = (f32[4,1,32,128]{3,2,1,0:T(8,128)S(1)}, f32[4,1,32,128]{3,2,1,0:T(8,128)S(1)}, u32[]{:S(2)}, u32[]{:S(2)}) collective-permute-start(f32[4,1,32,128]{3,2,1,0:T(8,128)S(1)} %get-tuple-element.143), channel_id=1, source_target_pairs={{4,0},{8,4},{12,8},{16,12},{20,16},{24,20},{28,24},{32,28},{36,32}... | collective-permute-start | bytes 196616 | tf_op jit(solution)/shard_map/ppermute | solution.py:23
  153.2 6.7 %collective-permute-start.20 = (f32[4,1,32,128]{3,2,1,0:T(8,128)S(1)}, f32[4,1,32,128]{3,2,1,0:T(8,128)S(1)}, u32[]{:S(2)}, u32[]{:S(2)}) collective-permute-start(f32[4,1,32,128]{3,2,1,0:T(8,128)S(1)} %get-tuple-element.142), channel_id=1, source_target_pairs={{0,4},{4,8},{8,12},{12,16},{16,20},{20,24},{24,28},{28,32},{32,36}... | collective-permute-start | bytes 196616 | tf_op jit(solution)/shard_map/ppermute | solution.py:20
  160.5 9.8 %collective-permute-start.23 = (f32[4,6,1,128]{3,2,1,0:T(1,128)}, f32[4,6,1,128]{3,2,1,0:T(1,128)}, u32[]{:S(2)}, u32[]{:S(2)}) collective-permute-start(f32[4,6,1,128]{3,2,1,0:T(1,128)} %get-tuple-element.113), channel_id=1, source_target_pairs={{1,0},{2,1},{3,2},{5,4},{6,5},{7,6},{9,8},{10,9},{11,10},{13,12},{... | collective-permute-start | bytes 36872 | tf_op jit(solution)/shard_map/ppermute | solution.py:23
  162.4 7.8 %collective-permute-start.22 = (f32[4,6,1,128]{3,2,1,0:T(1,128)}, f32[4,6,1,128]{3,2,1,0:T(1,128)}, u32[]{:S(2)}, u32[]{:S(2)}) collective-permute-start(f32[4,6,1,128]{3,2,1,0:T(1,128)} %get-tuple-element.112), channel_id=1, source_target_pairs={{0,1},{1,2},{2,3},{4,5},{5,6},{6,7},{8,9},{9,10},{10,11},{12,13},{... | collective-permute-start | bytes 36872 | tf_op jit(solution)/shard_map/ppermute | solution.py:20
  171.3 5.5 collective-permute-start.25
  172.6 5.0 collective-permute-start.24
  177.6 8.0 %collective-permute-start.27 = (f32[4,6,1,128]{3,2,1,0:T(1,128)S(1)}, f32[4,6,1,128]{3,2,1,0:T(1,128)S(1)}, u32[]{:S(2)}, u32[]{:S(2)}) collective-permute-start(f32[4,6,1,128]{3,2,1,0:T(1,128)S(1)} %get-tuple-element.111), channel_id=1, source_target_pairs={{1,0},{2,1},{3,2},{5,4},{6,5},{7,6},{9,8},{10,9},{11,10},{13,12},{... | collective-permute-start | bytes 36872 | tf_op jit(solution)/shard_map/ppermute | solution.py:23
  179.5 7.4 %collective-permute-start.26 = (f32[4,6,1,128]{3,2,1,0:T(1,128)S(1)}, f32[4,6,1,128]{3,2,1,0:T(1,128)S(1)}, u32[]{:S(2)}, u32[]{:S(2)}) collective-permute-start(f32[4,6,1,128]{3,2,1,0:T(1,128)S(1)} %get-tuple-element.110), channel_id=1, source_target_pairs={{0,1},{1,2},{2,3},{4,5},{5,6},{6,7},{8,9},{9,10},{10,11},{12,13},{... | collective-permute-start | bytes 36872 | tf_op jit(solution)/shard_map/ppermute | solution.py:20
  187.3 7.4 %collective-permute-start.29 = (f32[4,1,32,128]{3,2,1,0:T(8,128)S(1)}, f32[4,1,32,128]{3,2,1,0:T(8,128)S(1)}, u32[]{:S(2)}, u32[]{:S(2)}) collective-permute-start(f32[4,1,32,128]{3,2,1,0:T(8,128)S(1)} %get-tuple-element.139), channel_id=1, source_target_pairs={{4,0},{8,4},{12,8},{16,12},{20,16},{24,20},{28,24},{32,28},{36,32}... | collective-permute-start | bytes 196616 | tf_op jit(solution)/shard_map/ppermute | solution.py:23
  188.6 6.1 %collective-permute-start.28 = (f32[4,1,32,128]{3,2,1,0:T(8,128)S(1)}, f32[4,1,32,128]{3,2,1,0:T(8,128)S(1)}, u32[]{:S(2)}, u32[]{:S(2)}) collective-permute-start(f32[4,1,32,128]{3,2,1,0:T(8,128)S(1)} %get-tuple-element.138), channel_id=1, source_target_pairs={{0,4},{4,8},{8,12},{12,16},{16,20},{20,24},{24,28},{28,32},{32,36}... | collective-permute-start | bytes 196616 | tf_op jit(solution)/shard_map/ppermute | solution.py:20
  194.7 16.0 %collective-permute-start.31 = (f32[4,6,1,128]{3,2,1,0:T(1,128)S(1)}, f32[4,6,1,128]{3,2,1,0:T(1,128)S(1)}, u32[]{:S(2)}, u32[]{:S(2)}) collective-permute-start(f32[4,6,1,128]{3,2,1,0:T(1,128)S(1)} %get-tuple-element.109), channel_id=1, source_target_pairs={{1,0},{2,1},{3,2},{5,4},{6,5},{7,6},{9,8},{10,9},{11,10},{13,12},{... | collective-permute-start | bytes 36872 | tf_op jit(solution)/shard_map/ppermute | solution.py:23
  196.6 14.0 %collective-permute-start.30 = (f32[4,6,1,128]{3,2,1,0:T(1,128)S(1)}, f32[4,6,1,128]{3,2,1,0:T(1,128)S(1)}, u32[]{:S(2)}, u32[]{:S(2)}) collective-permute-start(f32[4,6,1,128]{3,2,1,0:T(1,128)S(1)} %get-tuple-element.108), channel_id=1, source_target_pairs={{0,1},{1,2},{2,3},{4,5},{5,6},{6,7},{8,9},{9,10},{10,11},{12,13},{... | collective-permute-start | bytes 36872 | tf_op jit(solution)/shard_map/ppermute | solution.py:20
  202.7 154.8 %collective-permute-start.35 = (f32[4,6,1,128]{3,2,1,0:T(1,128)S(1)}, f32[4,6,1,128]{3,2,1,0:T(1,128)S(1)}, u32[]{:S(2)}, u32[]{:S(2)}) collective-permute-start(f32[4,6,1,128]{3,2,1,0:T(1,128)S(1)} %get-tuple-element.107), channel_id=1, source_target_pairs={{1,0},{2,1},{3,2},{5,4},{6,5},{7,6},{9,8},{10,9},{11,10},{13,12},{... | collective-permute-start | bytes 36872 | tf_op jit(solution)/shard_map/ppermute | solution.py:23
  204.6 152.9 %collective-permute-start.34 = (f32[4,6,1,128]{3,2,1,0:T(1,128)S(1)}, f32[4,6,1,128]{3,2,1,0:T(1,128)S(1)}, u32[]{:S(2)}, u32[]{:S(2)}) collective-permute-start(f32[4,6,1,128]{3,2,1,0:T(1,128)S(1)} %get-tuple-element.106), channel_id=1, source_target_pairs={{0,1},{1,2},{2,3},{4,5},{5,6},{6,7},{8,9},{9,10},{10,11},{12,13},{... | collective-permute-start | bytes 36872 | tf_op jit(solution)/shard_map/ppermute | solution.py:20
  358.6 4.3 collective-permute-start.37
  359.9 3.9 collective-permute-start.36
  363.9 8.0 %collective-permute-start.39 = (f32[4,6,1,128]{3,2,1,0:T(1,128)S(1)}, f32[4,6,1,128]{3,2,1,0:T(1,128)S(1)}, u32[]{:S(2)}, u32[]{:S(2)}) collective-permute-start(f32[4,6,1,128]{3,2,1,0:T(1,128)S(1)} %get-tuple-element.105), channel_id=1, source_target_pairs={{1,0},{2,1},{3,2},{5,4},{6,5},{7,6},{9,8},{10,9},{11,10},{13,12},{... | collective-permute-start | bytes 36872 | tf_op jit(solution)/shard_map/ppermute | solution.py:23
  368.5 6.5 %collective-permute-start.38 = (f32[4,6,1,128]{3,2,1,0:T(1,128)S(1)}, f32[4,6,1,128]{3,2,1,0:T(1,128)S(1)}, u32[]{:S(2)}, u32[]{:S(2)}) collective-permute-start(f32[4,6,1,128]{3,2,1,0:T(1,128)S(1)} %get-tuple-element.104), channel_id=1, source_target_pairs={{0,1},{1,2},{2,3},{4,5},{5,6},{6,7},{8,9},{9,10},{10,11},{12,13},{... | collective-permute-start | bytes 36872 | tf_op jit(solution)/shard_map/ppermute | solution.py:20
  375.3 4.3 collective-permute-start.41
  380.6 8.0 %collective-permute-start.43 = (f32[4,6,1,128]{3,2,1,0:T(1,128)S(1)}, f32[4,6,1,128]{3,2,1,0:T(1,128)S(1)}, u32[]{:S(2)}, u32[]{:S(2)}) collective-permute-start(f32[4,6,1,128]{3,2,1,0:T(1,128)S(1)} %get-tuple-element.103), channel_id=1, source_target_pairs={{1,0},{2,1},{3,2},{5,4},{6,5},{7,6},{9,8},{10,9},{11,10},{13,12},{... | collective-permute-start | bytes 36872 | tf_op jit(solution)/shard_map/ppermute | solution.py:23
  382.5 7.4 %collective-permute-start.42 = (f32[4,6,1,128]{3,2,1,0:T(1,128)S(1)}, f32[4,6,1,128]{3,2,1,0:T(1,128)S(1)}, u32[]{:S(2)}, u32[]{:S(2)}) collective-permute-start(f32[4,6,1,128]{3,2,1,0:T(1,128)S(1)} %get-tuple-element.102), channel_id=1, source_target_pairs={{0,1},{1,2},{2,3},{4,5},{5,6},{6,7},{8,9},{9,10},{10,11},{12,13},{... | collective-permute-start | bytes 36872 | tf_op jit(solution)/shard_map/ppermute | solution.py:20
  390.2 5.4 collective-permute-start.45
  391.5 5.0 collective-permute-start.44
  396.6 8.2 %collective-permute-start.47 = (f32[4,6,1,128]{3,2,1,0:T(1,128)S(1)}, f32[4,6,1,128]{3,2,1,0:T(1,128)S(1)}, u32[]{:S(2)}, u32[]{:S(2)}) collective-permute-start(f32[4,6,1,128]{3,2,1,0:T(1,128)S(1)} %get-tuple-element.101), channel_id=1, source_target_pairs={{1,0},{2,1},{3,2},{5,4},{6,5},{7,6},{9,8},{10,9},{11,10},{13,12},{... | collective-permute-start | bytes 36872 | tf_op jit(solution)/shard_map/ppermute | solution.py:23
  398.5 7.4 %collective-permute-start.46 = (f32[4,6,1,128]{3,2,1,0:T(1,128)S(1)}, f32[4,6,1,128]{3,2,1,0:T(1,128)S(1)}, u32[]{:S(2)}, u32[]{:S(2)}) collective-permute-start(f32[4,6,1,128]{3,2,1,0:T(1,128)S(1)} %get-tuple-element.100), channel_id=1, source_target_pairs={{0,1},{1,2},{2,3},{4,5},{5,6},{6,7},{8,9},{9,10},{10,11},{12,13},{... | collective-permute-start | bytes 36872 | tf_op jit(solution)/shard_map/ppermute | solution.py:20
  406.2 7.2 %collective-permute-start.49 = (f32[4,1,32,128]{3,2,1,0:T(8,128)S(1)}, f32[4,1,32,128]{3,2,1,0:T(8,128)S(1)}, u32[]{:S(2)}, u32[]{:S(2)}) collective-permute-start(f32[4,1,32,128]{3,2,1,0:T(8,128)S(1)} %get-tuple-element.129), channel_id=1, source_target_pairs={{4,0},{8,4},{12,8},{16,12},{20,16},{24,20},{28,24},{32,28},{36,32}... | collective-permute-start | bytes 196616 | tf_op jit(solution)/shard_map/ppermute | solution.py:23
  407.5 6.8 %collective-permute-start.48 = (f32[4,1,32,128]{3,2,1,0:T(8,128)S(1)}, f32[4,1,32,128]{3,2,1,0:T(8,128)S(1)}, u32[]{:S(2)}, u32[]{:S(2)}) collective-permute-start(f32[4,1,32,128]{3,2,1,0:T(8,128)S(1)} %get-tuple-element.128), channel_id=1, source_target_pairs={{0,4},{4,8},{8,12},{12,16},{16,20},{20,24},{24,28},{28,32},{32,36}... | collective-permute-start | bytes 196616 | tf_op jit(solution)/shard_map/ppermute | solution.py:20
  414.3 8.0 %collective-permute-start.51 = (f32[4,6,1,128]{3,2,1,0:T(1,128)S(1)}, f32[4,6,1,128]{3,2,1,0:T(1,128)S(1)}, u32[]{:S(2)}, u32[]{:S(2)}) collective-permute-start(f32[4,6,1,128]{3,2,1,0:T(1,128)S(1)} %get-tuple-element.99), channel_id=1, source_target_pairs={{1,0},{2,1},{3,2},{5,4},{6,5},{7,6},{9,8},{10,9},{11,10},{13,12},{... | collective-permute-start | bytes 36872 | tf_op jit(solution)/shard_map/ppermute | solution.py:23
  416.3 7.4 %collective-permute-start.50 = (f32[4,6,1,128]{3,2,1,0:T(1,128)S(1)}, f32[4,6,1,128]{3,2,1,0:T(1,128)S(1)}, u32[]{:S(2)}, u32[]{:S(2)}) collective-permute-start(f32[4,6,1,128]{3,2,1,0:T(1,128)S(1)} %get-tuple-element.98), channel_id=1, source_target_pairs={{0,1},{1,2},{2,3},{4,5},{5,6},{6,7},{8,9},{9,10},{10,11},{12,13},{... | collective-permute-start | bytes 36872 | tf_op jit(solution)/shard_map/ppermute | solution.py:20
  424.0 6.9 %collective-permute-start.53 = (f32[4,1,32,128]{3,2,1,0:T(8,128)S(1)}, f32[4,1,32,128]{3,2,1,0:T(8,128)S(1)}, u32[]{:S(2)}, u32[]{:S(2)}) collective-permute-start(f32[4,1,32,128]{3,2,1,0:T(8,128)S(1)} %get-tuple-element.127), channel_id=1, source_target_pairs={{4,0},{8,4},{12,8},{16,12},{20,16},{24,20},{28,24},{32,28},{36,32}... | collective-permute-start | bytes 196616 | tf_op jit(solution)/shard_map/ppermute | solution.py:23
  425.3 6.5 %collective-permute-start.52 = (f32[4,1,32,128]{3,2,1,0:T(8,128)S(1)}, f32[4,1,32,128]{3,2,1,0:T(8,128)S(1)}, u32[]{:S(2)}, u32[]{:S(2)}) collective-permute-start(f32[4,1,32,128]{3,2,1,0:T(8,128)S(1)} %get-tuple-element.126), channel_id=1, source_target_pairs={{0,4},{4,8},{8,12},{12,16},{16,20},{20,24},{24,28},{28,32},{32,36}... | collective-permute-start | bytes 196616 | tf_op jit(solution)/shard_map/ppermute | solution.py:20
  431.8 8.0 %collective-permute-start.55 = (f32[4,6,1,128]{3,2,1,0:T(1,128)S(1)}, f32[4,6,1,128]{3,2,1,0:T(1,128)S(1)}, u32[]{:S(2)}, u32[]{:S(2)}) collective-permute-start(f32[4,6,1,128]{3,2,1,0:T(1,128)S(1)} %get-tuple-element.97), channel_id=1, source_target_pairs={{1,0},{2,1},{3,2},{5,4},{6,5},{7,6},{9,8},{10,9},{11,10},{13,12},{... | collective-permute-start | bytes 36872 | tf_op jit(solution)/shard_map/ppermute | solution.py:23
  433.7 7.4 %collective-permute-start.54 = (f32[4,6,1,128]{3,2,1,0:T(1,128)S(1)}, f32[4,6,1,128]{3,2,1,0:T(1,128)S(1)}, u32[]{:S(2)}, u32[]{:S(2)}) collective-permute-start(f32[4,6,1,128]{3,2,1,0:T(1,128)S(1)} %get-tuple-element.96), channel_id=1, source_target_pairs={{0,1},{1,2},{2,3},{4,5},{5,6},{6,7},{8,9},{9,10},{10,11},{12,13},{... | collective-permute-start | bytes 36872 | tf_op jit(solution)/shard_map/ppermute | solution.py:20
  441.5 6.9 %collective-permute-start.57 = (f32[4,1,32,128]{3,2,1,0:T(8,128)S(1)}, f32[4,1,32,128]{3,2,1,0:T(8,128)S(1)}, u32[]{:S(2)}, u32[]{:S(2)}) collective-permute-start(f32[4,1,32,128]{3,2,1,0:T(8,128)S(1)} %get-tuple-element.125), channel_id=1, source_target_pairs={{4,0},{8,4},{12,8},{16,12},{20,16},{24,20},{28,24},{32,28},{36,32}... | collective-permute-start | bytes 196616 | tf_op jit(solution)/shard_map/ppermute | solution.py:23
  442.8 6.5 %collective-permute-start.56 = (f32[4,1,32,128]{3,2,1,0:T(8,128)S(1)}, f32[4,1,32,128]{3,2,1,0:T(8,128)S(1)}, u32[]{:S(2)}, u32[]{:S(2)}) collective-permute-start(f32[4,1,32,128]{3,2,1,0:T(8,128)S(1)} %get-tuple-element.124), channel_id=1, source_target_pairs={{0,4},{4,8},{8,12},{12,16},{16,20},{20,24},{24,28},{28,32},{32,36}... | collective-permute-start | bytes 196616 | tf_op jit(solution)/shard_map/ppermute | solution.py:20
  449.3 8.0 %collective-permute-start.59 = (f32[4,6,1,128]{3,2,1,0:T(1,128)S(1)}, f32[4,6,1,128]{3,2,1,0:T(1,128)S(1)}, u32[]{:S(2)}, u32[]{:S(2)}) collective-permute-start(f32[4,6,1,128]{3,2,1,0:T(1,128)S(1)} %get-tuple-element.95), channel_id=1, source_target_pairs={{1,0},{2,1},{3,2},{5,4},{6,5},{7,6},{9,8},{10,9},{11,10},{13,12},{... | collective-permute-start | bytes 36872 | tf_op jit(solution)/shard_map/ppermute | solution.py:23
  451.2 7.4 %collective-permute-start.58 = (f32[4,6,1,128]{3,2,1,0:T(1,128)S(1)}, f32[4,6,1,128]{3,2,1,0:T(1,128)S(1)}, u32[]{:S(2)}, u32[]{:S(2)}) collective-permute-start(f32[4,6,1,128]{3,2,1,0:T(1,128)S(1)} %get-tuple-element.94), channel_id=1, source_target_pairs={{0,1},{1,2},{2,3},{4,5},{5,6},{6,7},{8,9},{9,10},{10,11},{12,13},{... | collective-permute-start | bytes 36872 | tf_op jit(solution)/shard_map/ppermute | solution.py:20
  459.1 7.1 %collective-permute-start.61 = (f32[8,1,32,128]{3,2,1,0:T(8,128)S(1)}, f32[8,1,32,128]{3,2,1,0:T(8,128)S(1)}, u32[]{:S(2)}, u32[]{:S(2)}) collective-permute-start(f32[8,1,32,128]{3,2,1,0:T(8,128)S(1)} %get-tuple-element.91), channel_id=1, source_target_pairs={{4,0},{8,4},{12,8},{16,12},{20,16},{24,20},{28,24},{32,28},{36,32}... | collective-permute-start | bytes 393224 | tf_op jit(solution)/shard_map/ppermute | solution.py:23
  460.4 6.7 %collective-permute-start.60 = (f32[8,1,32,128]{3,2,1,0:T(8,128)S(1)}, f32[8,1,32,128]{3,2,1,0:T(8,128)S(1)}, u32[]{:S(2)}, u32[]{:S(2)}) collective-permute-start(f32[8,1,32,128]{3,2,1,0:T(8,128)S(1)} %get-tuple-element.90), channel_id=1, source_target_pairs={{0,4},{4,8},{8,12},{12,16},{16,20},{20,24},{24,28},{28,32},{32,36}... | collective-permute-start | bytes 393224 | tf_op jit(solution)/shard_map/ppermute | solution.py:20
  467.2 8.8 %collective-permute-start.63 = (f32[8,6,1,128]{3,2,1,0:T(1,128)S(1)}, f32[8,6,1,128]{3,2,1,0:T(1,128)S(1)}, u32[]{:S(2)}, u32[]{:S(2)}) collective-permute-start(f32[8,6,1,128]{3,2,1,0:T(1,128)S(1)} %get-tuple-element.83), channel_id=1, source_target_pairs={{1,0},{2,1},{3,2},{5,4},{6,5},{7,6},{9,8},{10,9},{11,10},{13,12},{... | collective-permute-start | bytes 73736 | tf_op jit(solution)/shard_map/ppermute | solution.py:23
  469.2 7.5 %collective-permute-start.62 = (f32[8,6,1,128]{3,2,1,0:T(1,128)S(1)}, f32[8,6,1,128]{3,2,1,0:T(1,128)S(1)}, u32[]{:S(2)}, u32[]{:S(2)}) collective-permute-start(f32[8,6,1,128]{3,2,1,0:T(1,128)S(1)} %get-tuple-element.82), channel_id=1, source_target_pairs={{0,1},{1,2},{2,3},{4,5},{5,6},{6,7},{8,9},{9,10},{10,11},{12,13},{... | collective-permute-start | bytes 73736 | tf_op jit(solution)/shard_map/ppermute | solution.py:20
  (22 other events, 714.6 us)
Sparse Core Ops, SparseCore 0:
  477.9 105.9 all-reduce.20
where the time goes:
time: 595 us; the launch traced here: 592 us
  starting transfers between devices  224 us (38%)
  blocking collectives  174 us (29%)
  waiting for transfers between devices  153 us (26%)
  other arithmetic  15 us (3%)
  between operations  14.6 us (2%)
  local copies, waits for them, and re-layouts  12.1 us (2%)
    ppermute x32, starting transfers between devices, padded_2(): lax.ppermute(lax.slice_in_dim(block, block.shape[dim] - width, None, axis...  166 us
    psum x1, blocking collectives, body(): predicted = lax.psum(local_values, ('gx', 'gy'))  145 us
    psum x1, waiting for transfers between devices, reduce_groups(): summed = lax.psum(partial_value, 'src')  106 us
    ppermute x32, starting transfers between devices, padded_2(): lax.ppermute(lax.slice_in_dim(block, 0, width, axis=dim), axis, backward)  58.2 us
    all_gather x1, blocking collectives, body(): panel = lax.all_gather(conductivity, 'src', axis=2, tiled=True)  29 us
    ppermute x32, waiting for transfers between devices, padded_2(): lax.ppermute(lax.slice_in_dim(block, block.shape[dim] - width, None, axis...  24.7 us
    ppermute x32, waiting for transfers between devices, padded_2(): lax.ppermute(lax.slice_in_dim(block, 0, width, axis=dim), axis, backward)  22 us
  transfers between devices with their start and end apart: 65, of which 24 were waited for; matrix products, arithmetic and copies ran while one was open for 3% of the time, Pallas kernels for 0%

commit v1 on v0

--- a/solution.py
+++ b/solution.py
@@ -101,7 +101,9 @@
 
 
 def body(warm_potential, warm_adjoint, conductivity, electrodes, receivers, observed, source_order):
-    panel = lax.all_gather(conductivity, "src", axis=2, tiled=True)
+    panel = jnp.concatenate(
+        lax.all_to_all(jnp.stack([conductivity] * lax.axis_size("src")), "src", 0, 0), axis=2
+    )
     group = lax.axis_index("src")
     slots = warm_potential.shape[0]
     width_x = panel.shape[0]

time: 595 us -> 564 us (0.948)
  blocking collectives: 174 us -> 138 us
  waiting for transfers between devices: 153 us -> 186 us
  starting transfers between devices: 224 us -> 194 us
    ppermute x32, starting transfers between devices: 166 us -> 102 us  [padded_2(): lax.ppermute(lax.slice_in_dim(block, block.shape[dim] - width, None, axis...]
    ppermute x32, waiting for transfers between devices: 22 us -> 80.4 us  [padded_2(): lax.ppermute(lax.slice_in_dim(block, 0, width, axis=dim), axis, backward)]
    all_gather x1 -> x0, blocking collectives: 29 us -> none  [body(): panel = lax.all_gather(conductivity, 'src', axis=2, tiled=True)]
    ppermute x32, starting transfers between devices: 58.2 us -> 87.3 us  [padded_2(): lax.ppermute(lax.slice_in_dim(block, 0, width, axis=dim), axis, backward)]
    psum x1, waiting for transfers between devices: 106 us -> 90.8 us  [reduce_groups(): summed = lax.psum(partial_value, 'src')]
    ppermute x32, waiting for transfers between devices: 24.7 us -> 14.8 us  [padded_2(): lax.ppermute(lax.slice_in_dim(block, block.shape[dim] - width, None, axis...]
    psum x1, blocking collectives: 145 us -> 138 us  [body(): predicted = lax.psum(local_values, ('gx', 'gy'))]
  transfers between devices with their start and end apart: 65 -> 66, of which waited for: 24 -> 28; matrix products, arithmetic and copies ran while one was open for 3% -> 2% of each run, Pallas kernels for 0% -> 0%
where the time goes in v1:
time: 564 us; the launch traced here: 561 us
  starting transfers between devices  194 us (34%)
  waiting for transfers between devices  186 us (33%)
  blocking collectives  138 us (24%)
  between operations  14.7 us (3%)
  local copies, waits for them, and re-layouts  14.6 us (3%)
  other arithmetic  12.8 us (2%)
    psum x1, blocking collectives, body(): predicted = lax.psum(local_values, ('gx', 'gy'))  138 us
    ppermute x32, starting transfers between devices, padded_2(): lax.ppermute(lax.slice_in_dim(block, block.shape[dim] - width, None, axis...  102 us
    psum x1, waiting for transfers between devices, reduce_groups(): summed = lax.psum(partial_value, 'src')  90.8 us
    ppermute x32, starting transfers between devices, padded_2(): lax.ppermute(lax.slice_in_dim(block, 0, width, axis=dim), axis, backward)  87.3 us
    ppermute x32, waiting for transfers between devices, padded_2(): lax.ppermute(lax.slice_in_dim(block, 0, width, axis=dim), axis, backward)  80.4 us
    ppermute x32, waiting for transfers between devices, padded_2(): lax.ppermute(lax.slice_in_dim(block, block.shape[dim] - width, None, axis...  14.8 us
  transfers between devices with their start and end apart: 66, of which 28 were waited for; matrix products, arithmetic and copies ran while one was open for 2% of the time, Pallas kernels for 0%

profile of v1, /device:TPU:16, one launch (start us, length us, event | category | flops | bytes accessed | tf_op | source)
XLA Modules:
  0.0 561.4 jit_solution(571138566933516642)
XLA Ops:
  8.1 5.3 all-to-all-start
  22.1 5.2 collective-permute-start
  28.7 4.8 collective-permute-start.6
  33.5 1.9 collective-permute-start.7
  35.7 6.0 %collective-permute-start.2 = (f32[1,6,1,128]{2,3,1,0:T(8,128)S(1)}, f32[1,6,1,128]{2,3,1,0:T(8,128)S(1)}, u32[]{:S(2)}, u32[]{:S(2)}) collective-permute-start(f32[1,6,1,128]{2,3,1,0:T(8,128)S(1)} %get-tuple-element.124), channel_id=1, source_target_pairs={{0,1},{1,2},{2,3},{4,5},{5,6},{6,7},{8,9},{9,10},{10,11},{12,13},{... | collective-permute-start | bytes 9224 | tf_op jit(solution)/shard_map/ppermute | solution.py:20
  41.8 1.9 collective-permute-start.3
  43.9 14.7 %collective-permute-done.2 = f32[1,6,1,128]{2,3,1,0:T(8,128)S(1)} collective-permute-done((f32[1,6,1,128]{2,3,1,0:T(8,128)S(1)}, f32[1,6,1,128]{2,3,1,0:T(8,128)S(1)}, u32[]{:S(2)}, u32[]{:S(2)}) %collective-permute-start.2) | collective-permute-done | bytes 3104 | tf_op jit(solution)/shard_map/ppermute | solution.py:20
  58.7 5.4 collective-permute-done.3
  68.7 2.2 collective-permute-start.8
  72.3 4.8 collective-permute-done.9
  77.1 2.4 collective-permute-start.10
  79.6 4.3 collective-permute-start.11
  83.9 3.3 collective-permute-done.11
  87.6 3.4 collective-permute-start.12
  92.3 2.7 collective-permute-done.13
  95.0 1.9 collective-permute-start.14
  97.0 4.8 collective-permute-start.15
  101.8 2.9 collective-permute-done.15
  105.0 3.8 collective-permute-start.16
  110.1 2.9 collective-permute-done.17
  115.0 4.8 collective-permute-start.19
  120.5 4.9 collective-permute-start.32
  127.0 3.0 collective-permute-start.20
  132.0 2.6 collective-permute-done.21
  135.2 3.4 collective-permute-start.22
  138.6 3.3 collective-permute-start.23
  143.1 3.4 collective-permute-done.23
  146.8 3.4 collective-permute-start.24
  152.4 3.1 collective-permute-done.25
  157.4 4.8 collective-permute-start.27
  162.3 2.8 collective-permute-done.27
  165.4 3.7 collective-permute-start.28
  171.3 2.7 collective-permute-done.29
  176.0 4.8 collective-permute-start.31
  180.8 3.1 collective-permute-start.34
  184.0 3.6 collective-permute-start.35
  189.2 138.5 %psum.14 = f32[4,128]{1,0:T(4,128)S(1)} all-reduce(f32[4,128]{1,0:T(4,128)S(1)} %fusion.304), channel_id=1, replica_groups=mesh['src'=8,'gx'=16,'gy'=4] {'gx','gy'}, use_global_device_ids=true, to_apply=%region_0.1 | all-reduce | flops 512 | bytes 4096 | tf_op jit(solution)/shard_map/psum | solution.py:142
  333.9 3.6 collective-permute-start.38
  337.5 3.1 collective-permute-start.39
  340.7 4.5 collective-permute-done.39
  351.9 4.8 collective-permute-start.43
  356.8 2.9 collective-permute-done.43
  359.9 3.3 collective-permute-start.44
  364.5 7.7 %collective-permute-done.45 = f32[4,1,32,128]{3,2,1,0:T(8,128)S(1)} collective-permute-done((f32[4,1,32,128]{3,2,1,0:T(8,128)S(1)}, f32[4,1,32,128]{3,2,1,0:T(8,128)S(1)}, u32[]{:S(2)}, u32[]{:S(2)}) %collective-permute-start.45) | collective-permute-done | bytes 65568 | tf_op jit(solution)/shard_map/ppermute | solution.py:23
  372.2 1.9 collective-permute-start.46
  374.1 4.8 collective-permute-start.47
  379.0 2.9 collective-permute-done.47
  382.1 7.3 %collective-permute-start.48 = (f32[4,1,32,128]{3,2,1,0:T(8,128)S(1)}, f32[4,1,32,128]{3,2,1,0:T(8,128)S(1)}, u32[]{:S(2)}, u32[]{:S(2)}) collective-permute-start(f32[4,1,32,128]{3,2,1,0:T(8,128)S(1)} %get-tuple-element.130), channel_id=1, source_target_pairs={{0,4},{4,8},{8,12},{12,16},{16,20},{20,24},{24,28},{28,32},{32,36}... | collective-permute-start | bytes 196616 | tf_op jit(solution)/shard_map/ppermute | solution.py:20
  390.7 4.2 collective-permute-done.49
  395.0 1.9 collective-permute-start.50
  396.9 5.0 collective-permute-start.51
  401.9 2.7 collective-permute-done.51
  404.9 4.8 collective-permute-start.52
  411.0 2.6 collective-permute-done.53
  415.5 4.8 collective-permute-start.55
  420.4 2.9 collective-permute-done.55
  423.6 5.1 collective-permute-start.56
  429.9 2.5 collective-permute-done.57
  434.3 4.8 collective-permute-start.59
  439.2 2.9 collective-permute-done.59
  442.5 4.9 collective-permute-start.60
  448.7 2.6 collective-permute-done.61
  453.2 4.8 collective-permute-start.63
  462.2 90.8 %all-reduce.21.cloned.1.call-done = f32[4,32,128]{2,1,0:T(8,128)} async-done(((f32[4,32,128]{2,1,0:T(8,128)}), f32[4,32,128]{2,1,0:T(8,128)}) %all-reduce.21.cloned.1.call-update) | async-done | bytes 65552 | tf_op jit(solution)/shard_map/psum | solution.py:99
  (213 shorter events, 71.8 us)
Async XLA Ops:
  8.1 12.5 %all-to-all-start = ((f32[8,1,2048]{2,1,0:T(1,128)}), f32[8,1,2048]{2,1,0:T(1,128)S(1)}, u32[]{:S(2)}, u32[]{:S(2)}) async-start(f32[8,1,2048]{2,1,0:T(1,128)} %reshape.188), calls=%async_computation | async-start | bytes 131072 | tf_op jit(solution)/shard_map/all_to_all | solution.py:105
  13.4 539.5 %all-reduce.21.cloned.1.call-start = ((), (), s32[]{:S(2)}) async-start(), calls=%async_computation.1 | async-start | bytes 131072 | tf_op jit(solution)/shard_map/psum | solution.py:99
  13.5 6.8 %collective-permute-start.4 = (f32[4,1,32,128]{3,2,1,0:T(8,128)S(1)}, f32[4,1,32,128]{3,2,1,0:T(8,128)S(1)}, u32[]{:S(2)}, u32[]{:S(2)}) collective-permute-start(f32[4,1,32,128]{3,2,1,0:T(8,128)S(1)} %get-tuple-element.153), channel_id=1, source_target_pairs={{0,4},{4,8},{8,12},{12,16},{16,20},{20,24},{24,28},{28,32},{32,36}... | collective-permute-start | bytes 196616 | tf_op jit(solution)/shard_map/ppermute | solution.py:20
  15.0 5.6 collective-permute-start.5
  22.1 13.4 %collective-permute-start = (f32[1,1,32,128]{2,3,1,0:T(8,128)S(1)}, f32[1,1,32,128]{2,3,1,0:T(8,128)S(1)}, u32[]{:S(2)}, u32[]{:S(2)}) collective-permute-start(f32[1,1,32,128]{2,3,1,0:T(8,128)S(1)} %get-tuple-element.156), channel_id=1, source_target_pairs={{0,4},{4,8},{8,12},{12,16},{16,20},{20,24},{24,28},{28,32},{32,36}... | collective-permute-start | bytes 49160 | tf_op jit(solution)/shard_map/ppermute | solution.py:20
  27.4 8.1 %collective-permute-start.1 = (f32[1,1,32,128]{2,3,1,0:T(8,128)S(1)}, f32[1,1,32,128]{2,3,1,0:T(8,128)S(1)}, u32[]{:S(2)}, u32[]{:S(2)}) collective-permute-start(f32[1,1,32,128]{2,3,1,0:T(8,128)S(1)} %get-tuple-element.157), channel_id=1, source_target_pairs={{4,0},{8,4},{12,8},{16,12},{20,16},{24,20},{28,24},{32,28},{36,32}... | collective-permute-start | bytes 49160 | tf_op jit(solution)/shard_map/ppermute | solution.py:23
  28.7 38.9 %collective-permute-start.6 = (f32[4,6,1,128]{3,2,1,0:T(1,128)S(1)}, f32[4,6,1,128]{3,2,1,0:T(1,128)S(1)}, u32[]{:S(2)}, u32[]{:S(2)}) collective-permute-start(f32[4,6,1,128]{3,2,1,0:T(1,128)S(1)} %get-tuple-element.122), channel_id=1, source_target_pairs={{0,1},{1,2},{2,3},{4,5},{5,6},{6,7},{8,9},{9,10},{10,11},{12,13},{... | collective-permute-start | bytes 36872 | tf_op jit(solution)/shard_map/ppermute | solution.py:20
  33.5 34.1 %collective-permute-start.7 = (f32[4,6,1,128]{3,2,1,0:T(1,128)S(1)}, f32[4,6,1,128]{3,2,1,0:T(1,128)S(1)}, u32[]{:S(2)}, u32[]{:S(2)}) collective-permute-start(f32[4,6,1,128]{3,2,1,0:T(1,128)S(1)} %get-tuple-element.123), channel_id=1, source_target_pairs={{1,0},{2,1},{3,2},{5,4},{6,5},{7,6},{9,8},{10,9},{11,10},{13,12},{... | collective-permute-start | bytes 36872 | tf_op jit(solution)/shard_map/ppermute | solution.py:23
  35.7 22.9 %collective-permute-start.2 = (f32[1,6,1,128]{2,3,1,0:T(8,128)S(1)}, f32[1,6,1,128]{2,3,1,0:T(8,128)S(1)}, u32[]{:S(2)}, u32[]{:S(2)}) collective-permute-start(f32[1,6,1,128]{2,3,1,0:T(8,128)S(1)} %get-tuple-element.124), channel_id=1, source_target_pairs={{0,1},{1,2},{2,3},{4,5},{5,6},{6,7},{8,9},{9,10},{10,11},{12,13},{... | collective-permute-start | bytes 9224 | tf_op jit(solution)/shard_map/ppermute | solution.py:20
  41.8 22.3 %collective-permute-start.3 = (f32[1,6,1,128]{2,3,1,0:T(8,128)S(1)}, f32[1,6,1,128]{2,3,1,0:T(8,128)S(1)}, u32[]{:S(2)}, u32[]{:S(2)}) collective-permute-start(f32[1,6,1,128]{2,3,1,0:T(8,128)S(1)} %get-tuple-element.125), channel_id=1, source_target_pairs={{1,0},{2,1},{3,2},{5,4},{6,5},{7,6},{9,8},{10,9},{11,10},{13,12},{... | collective-permute-start | bytes 9224 | tf_op jit(solution)/shard_map/ppermute | solution.py:23
  68.7 3.5 collective-permute-start.8
  71.0 6.2 %collective-permute-start.9 = (f32[4,1,32,128]{3,2,1,0:T(8,128)S(1)}, f32[4,1,32,128]{3,2,1,0:T(8,128)S(1)}, u32[]{:S(2)}, u32[]{:S(2)}) collective-permute-start(f32[4,1,32,128]{3,2,1,0:T(8,128)S(1)} %get-tuple-element.151), channel_id=1, source_target_pairs={{4,0},{8,4},{12,8},{16,12},{20,16},{24,20},{28,24},{32,28},{36,32}... | collective-permute-start | bytes 196616 | tf_op jit(solution)/shard_map/ppermute | solution.py:23
  77.1 6.8 %collective-permute-start.10 = (f32[4,6,1,128]{3,2,1,0:T(1,128)S(1)}, f32[4,6,1,128]{3,2,1,0:T(1,128)S(1)}, u32[]{:S(2)}, u32[]{:S(2)}) collective-permute-start(f32[4,6,1,128]{3,2,1,0:T(1,128)S(1)} %get-tuple-element.120), channel_id=1, source_target_pairs={{0,1},{1,2},{2,3},{4,5},{5,6},{6,7},{8,9},{9,10},{10,11},{12,13},{... | collective-permute-start | bytes 36872 | tf_op jit(solution)/shard_map/ppermute | solution.py:20
  79.6 7.7 %collective-permute-start.11 = (f32[4,6,1,128]{3,2,1,0:T(1,128)S(1)}, f32[4,6,1,128]{3,2,1,0:T(1,128)S(1)}, u32[]{:S(2)}, u32[]{:S(2)}) collective-permute-start(f32[4,6,1,128]{3,2,1,0:T(1,128)S(1)} %get-tuple-element.121), channel_id=1, source_target_pairs={{1,0},{2,1},{3,2},{5,4},{6,5},{7,6},{9,8},{10,9},{11,10},{13,12},{... | collective-permute-start | bytes 36872 | tf_op jit(solution)/shard_map/ppermute | solution.py:23
  87.6 4.7 collective-permute-start.12
  91.0 4.0 collective-permute-start.13
  95.0 6.8 %collective-permute-start.14 = (f32[4,6,1,128]{3,2,1,0:T(1,128)S(1)}, f32[4,6,1,128]{3,2,1,0:T(1,128)S(1)}, u32[]{:S(2)}, u32[]{:S(2)}) collective-permute-start(f32[4,6,1,128]{3,2,1,0:T(1,128)S(1)} %get-tuple-element.118), channel_id=1, source_target_pairs={{0,1},{1,2},{2,3},{4,5},{5,6},{6,7},{8,9},{9,10},{10,11},{12,13},{... | collective-permute-start | bytes 36872 | tf_op jit(solution)/shard_map/ppermute | solution.py:20
  97.0 7.7 %collective-permute-start.15 = (f32[4,6,1,128]{3,2,1,0:T(1,128)S(1)}, f32[4,6,1,128]{3,2,1,0:T(1,128)S(1)}, u32[]{:S(2)}, u32[]{:S(2)}) collective-permute-start(f32[4,6,1,128]{3,2,1,0:T(1,128)S(1)} %get-tuple-element.119), channel_id=1, source_target_pairs={{1,0},{2,1},{3,2},{5,4},{6,5},{7,6},{9,8},{10,9},{11,10},{13,12},{... | collective-permute-start | bytes 36872 | tf_op jit(solution)/shard_map/ppermute | solution.py:23
  105.0 5.2 collective-permute-start.16
  108.8 4.2 collective-permute-start.17
  113.0 13.7 %collective-permute-start.18 = (f32[4,6,1,128]{3,2,1,0:T(1,128)S(1)}, f32[4,6,1,128]{3,2,1,0:T(1,128)S(1)}, u32[]{:S(2)}, u32[]{:S(2)}) collective-permute-start(f32[4,6,1,128]{3,2,1,0:T(1,128)S(1)} %get-tuple-element.116), channel_id=1, source_target_pairs={{0,1},{1,2},{2,3},{4,5},{5,6},{6,7},{8,9},{9,10},{10,11},{12,13},{... | collective-permute-start | bytes 36872 | tf_op jit(solution)/shard_map/ppermute | solution.py:20
  115.0 11.8 %collective-permute-start.19 = (f32[4,6,1,128]{3,2,1,0:T(1,128)S(1)}, f32[4,6,1,128]{3,2,1,0:T(1,128)S(1)}, u32[]{:S(2)}, u32[]{:S(2)}) collective-permute-start(f32[4,6,1,128]{3,2,1,0:T(1,128)S(1)} %get-tuple-element.117), channel_id=1, source_target_pairs={{1,0},{2,1},{3,2},{5,4},{6,5},{7,6},{9,8},{10,9},{11,10},{13,12},{... | collective-permute-start | bytes 36872 | tf_op jit(solution)/shard_map/ppermute | solution.py:23
  120.5 31.0 %collective-permute-start.32 = (f32[4,1,32,128]{3,2,1,0:T(8,128)}, f32[4,1,32,128]{3,2,1,0:T(8,128)}, u32[]{:S(2)}, u32[]{:S(2)}) collective-permute-start(f32[4,1,32,128]{3,2,1,0:T(8,128)} %get-tuple-element.139), channel_id=1, source_target_pairs={{0,4},{4,8},{8,12},{12,16},{16,20},{20,24},{24,28},{28,32},{32,36}... | collective-permute-start | bytes 196616 | tf_op jit(solution)/shard_map/ppermute | solution.py:20
  125.4 45.0 %collective-permute-start.33 = (f32[4,1,32,128]{3,2,1,0:T(8,128)}, f32[4,1,32,128]{3,2,1,0:T(8,128)}, u32[]{:S(2)}, u32[]{:S(2)}) collective-permute-start(f32[4,1,32,128]{3,2,1,0:T(8,128)} %get-tuple-element.138), channel_id=1, source_target_pairs={{4,0},{8,4},{12,8},{16,12},{20,16},{24,20},{28,24},{32,28},{36,32}... | collective-permute-start | bytes 196616 | tf_op jit(solution)/shard_map/ppermute | solution.py:23
  127.0 4.9 collective-permute-start.20
  130.1 4.4 collective-permute-start.21
  135.2 8.0 %collective-permute-start.22 = (f32[4,6,1,128]{3,2,1,0:T(1,128)}, f32[4,6,1,128]{3,2,1,0:T(1,128)S(1)}, u32[]{:S(2)}, u32[]{:S(2)}) collective-permute-start(f32[4,6,1,128]{3,2,1,0:T(1,128)} %get-tuple-element.114), channel_id=1, source_target_pairs={{0,1},{1,2},{2,3},{4,5},{5,6},{6,7},{8,9},{9,10},{10,11},{12,13},{... | collective-permute-start | bytes 36872 | tf_op jit(solution)/shard_map/ppermute | solution.py:20
  138.6 7.9 %collective-permute-start.23 = (f32[4,6,1,128]{3,2,1,0:T(1,128)}, f32[4,6,1,128]{3,2,1,0:T(1,128)S(1)}, u32[]{:S(2)}, u32[]{:S(2)}) collective-permute-start(f32[4,6,1,128]{3,2,1,0:T(1,128)} %get-tuple-element.115), channel_id=1, source_target_pairs={{1,0},{2,1},{3,2},{5,4},{6,5},{7,6},{9,8},{10,9},{11,10},{13,12},{... | collective-permute-start | bytes 36872 | tf_op jit(solution)/shard_map/ppermute | solution.py:23
  146.8 5.6 collective-permute-start.24
  150.2 5.3 collective-permute-start.25
  155.5 6.8 %collective-permute-start.26 = (f32[4,6,1,128]{3,2,1,0:T(1,128)S(1)}, f32[4,6,1,128]{3,2,1,0:T(1,128)S(1)}, u32[]{:S(2)}, u32[]{:S(2)}) collective-permute-start(f32[4,6,1,128]{3,2,1,0:T(1,128)S(1)} %get-tuple-element.112), channel_id=1, source_target_pairs={{0,1},{1,2},{2,3},{4,5},{5,6},{6,7},{8,9},{9,10},{10,11},{12,13},{... | collective-permute-start | bytes 36872 | tf_op jit(solution)/shard_map/ppermute | solution.py:20
  157.4 7.7 %collective-permute-start.27 = (f32[4,6,1,128]{3,2,1,0:T(1,128)S(1)}, f32[4,6,1,128]{3,2,1,0:T(1,128)S(1)}, u32[]{:S(2)}, u32[]{:S(2)}) collective-permute-start(f32[4,6,1,128]{3,2,1,0:T(1,128)S(1)} %get-tuple-element.113), channel_id=1, source_target_pairs={{1,0},{2,1},{3,2},{5,4},{6,5},{7,6},{9,8},{10,9},{11,10},{13,12},{... | collective-permute-start | bytes 36872 | tf_op jit(solution)/shard_map/ppermute | solution.py:23
  165.4 5.9 %collective-permute-start.28 = (f32[4,1,32,128]{3,2,1,0:T(8,128)S(1)}, f32[4,1,32,128]{3,2,1,0:T(8,128)S(1)}, u32[]{:S(2)}, u32[]{:S(2)}) collective-permute-start(f32[4,1,32,128]{3,2,1,0:T(8,128)S(1)} %get-tuple-element.140), channel_id=1, source_target_pairs={{0,4},{4,8},{8,12},{12,16},{16,20},{20,24},{24,28},{28,32},{32,36}... | collective-permute-start | bytes 196616 | tf_op jit(solution)/shard_map/ppermute | solution.py:20
  169.1 4.9 collective-permute-start.29
  174.1 13.5 %collective-permute-start.30 = (f32[4,6,1,128]{3,2,1,0:T(1,128)S(1)}, f32[4,6,1,128]{3,2,1,0:T(1,128)S(1)}, u32[]{:S(2)}, u32[]{:S(2)}) collective-permute-start(f32[4,6,1,128]{3,2,1,0:T(1,128)S(1)} %get-tuple-element.110), channel_id=1, source_target_pairs={{0,1},{1,2},{2,3},{4,5},{5,6},{6,7},{8,9},{9,10},{10,11},{12,13},{... | collective-permute-start | bytes 36872 | tf_op jit(solution)/shard_map/ppermute | solution.py:20
  176.0 11.6 %collective-permute-start.31 = (f32[4,6,1,128]{3,2,1,0:T(1,128)S(1)}, f32[4,6,1,128]{3,2,1,0:T(1,128)S(1)}, u32[]{:S(2)}, u32[]{:S(2)}) collective-permute-start(f32[4,6,1,128]{3,2,1,0:T(1,128)S(1)} %get-tuple-element.111), channel_id=1, source_target_pairs={{1,0},{2,1},{3,2},{5,4},{6,5},{7,6},{9,8},{10,9},{11,10},{13,12},{... | collective-permute-start | bytes 36872 | tf_op jit(solution)/shard_map/ppermute | solution.py:23
  180.8 147.4 %collective-permute-start.34 = (f32[4,6,1,128]{3,2,1,0:T(1,128)S(1)}, f32[4,6,1,128]{3,2,1,0:T(1,128)S(1)}, u32[]{:S(2)}, u32[]{:S(2)}) collective-permute-start(f32[4,6,1,128]{3,2,1,0:T(1,128)S(1)} %get-tuple-element.108), channel_id=1, source_target_pairs={{0,1},{1,2},{2,3},{4,5},{5,6},{6,7},{8,9},{9,10},{10,11},{12,13},{... | collective-permute-start | bytes 36872 | tf_op jit(solution)/shard_map/ppermute | solution.py:20
  184.0 144.3 %collective-permute-start.35 = (f32[4,6,1,128]{3,2,1,0:T(1,128)S(1)}, f32[4,6,1,128]{3,2,1,0:T(1,128)S(1)}, u32[]{:S(2)}, u32[]{:S(2)}) collective-permute-start(f32[4,6,1,128]{3,2,1,0:T(1,128)S(1)} %get-tuple-element.109), channel_id=1, source_target_pairs={{1,0},{2,1},{3,2},{5,4},{6,5},{7,6},{9,8},{10,9},{11,10},{13,12},{... | collective-permute-start | bytes 36872 | tf_op jit(solution)/shard_map/ppermute | solution.py:23
  330.7 3.1 collective-permute-start.37
  333.9 6.8 %collective-permute-start.38 = (f32[4,6,1,128]{3,2,1,0:T(1,128)S(1)}, f32[4,6,1,128]{3,2,1,0:T(1,128)S(1)}, u32[]{:S(2)}, u32[]{:S(2)}) collective-permute-start(f32[4,6,1,128]{3,2,1,0:T(1,128)S(1)} %get-tuple-element.106), channel_id=1, source_target_pairs={{0,1},{1,2},{2,3},{4,5},{5,6},{6,7},{8,9},{9,10},{10,11},{12,13},{... | collective-permute-start | bytes 36872 | tf_op jit(solution)/shard_map/ppermute | solution.py:20
  337.5 7.7 %collective-permute-start.39 = (f32[4,6,1,128]{3,2,1,0:T(1,128)S(1)}, f32[4,6,1,128]{3,2,1,0:T(1,128)S(1)}, u32[]{:S(2)}, u32[]{:S(2)}) collective-permute-start(f32[4,6,1,128]{3,2,1,0:T(1,128)S(1)} %get-tuple-element.107), channel_id=1, source_target_pairs={{1,0},{2,1},{3,2},{5,4},{6,5},{7,6},{9,8},{10,9},{11,10},{13,12},{... | collective-permute-start | bytes 36872 | tf_op jit(solution)/shard_map/ppermute | solution.py:23
  346.8 3.1 collective-permute-start.41
  350.0 6.8 %collective-permute-start.42 = (f32[4,6,1,128]{3,2,1,0:T(1,128)S(1)}, f32[4,6,1,128]{3,2,1,0:T(1,128)S(1)}, u32[]{:S(2)}, u32[]{:S(2)}) collective-permute-start(f32[4,6,1,128]{3,2,1,0:T(1,128)S(1)} %get-tuple-element.104), channel_id=1, source_target_pairs={{0,1},{1,2},{2,3},{4,5},{5,6},{6,7},{8,9},{9,10},{10,11},{12,13},{... | collective-permute-start | bytes 36872 | tf_op jit(solution)/shard_map/ppermute | solution.py:20
  351.9 7.7 %collective-permute-start.43 = (f32[4,6,1,128]{3,2,1,0:T(1,128)S(1)}, f32[4,6,1,128]{3,2,1,0:T(1,128)S(1)}, u32[]{:S(2)}, u32[]{:S(2)}) collective-permute-start(f32[4,6,1,128]{3,2,1,0:T(1,128)S(1)} %get-tuple-element.105), channel_id=1, source_target_pairs={{1,0},{2,1},{3,2},{5,4},{6,5},{7,6},{9,8},{10,9},{11,10},{13,12},{... | collective-permute-start | bytes 36872 | tf_op jit(solution)/shard_map/ppermute | solution.py:23
  359.9 4.6 collective-permute-start.44
  363.2 9.0 %collective-permute-start.45 = (f32[4,1,32,128]{3,2,1,0:T(8,128)S(1)}, f32[4,1,32,128]{3,2,1,0:T(8,128)S(1)}, u32[]{:S(2)}, u32[]{:S(2)}) collective-permute-start(f32[4,1,32,128]{3,2,1,0:T(8,128)S(1)} %get-tuple-element.133), channel_id=1, source_target_pairs={{4,0},{8,4},{12,8},{16,12},{20,16},{24,20},{28,24},{32,28},{36,32}... | collective-permute-start | bytes 196616 | tf_op jit(solution)/shard_map/ppermute | solution.py:23
  372.2 6.8 %collective-permute-start.46 = (f32[4,6,1,128]{3,2,1,0:T(1,128)S(1)}, f32[4,6,1,128]{3,2,1,0:T(1,128)S(1)}, u32[]{:S(2)}, u32[]{:S(2)}) collective-permute-start(f32[4,6,1,128]{3,2,1,0:T(1,128)S(1)} %get-tuple-element.102), channel_id=1, source_target_pairs={{0,1},{1,2},{2,3},{4,5},{5,6},{6,7},{8,9},{9,10},{10,11},{12,13},{... | collective-permute-start | bytes 36872 | tf_op jit(solution)/shard_map/ppermute | solution.py:20
  374.1 7.7 %collective-permute-start.47 = (f32[4,6,1,128]{3,2,1,0:T(1,128)S(1)}, f32[4,6,1,128]{3,2,1,0:T(1,128)S(1)}, u32[]{:S(2)}, u32[]{:S(2)}) collective-permute-start(f32[4,6,1,128]{3,2,1,0:T(1,128)S(1)} %get-tuple-element.103), channel_id=1, source_target_pairs={{1,0},{2,1},{3,2},{5,4},{6,5},{7,6},{9,8},{10,9},{11,10},{13,12},{... | collective-permute-start | bytes 36872 | tf_op jit(solution)/shard_map/ppermute | solution.py:23
  382.1 8.6 %collective-permute-start.48 = (f32[4,1,32,128]{3,2,1,0:T(8,128)S(1)}, f32[4,1,32,128]{3,2,1,0:T(8,128)S(1)}, u32[]{:S(2)}, u32[]{:S(2)}) collective-permute-start(f32[4,1,32,128]{3,2,1,0:T(8,128)S(1)} %get-tuple-element.130), channel_id=1, source_target_pairs={{0,4},{4,8},{8,12},{12,16},{16,20},{20,24},{24,28},{28,32},{32,36}... | collective-permute-start | bytes 196616 | tf_op jit(solution)/shard_map/ppermute | solution.py:20
  389.4 5.5 collective-permute-start.49
  395.0 6.9 %collective-permute-start.50 = (f32[4,6,1,128]{3,2,1,0:T(1,128)S(1)}, f32[4,6,1,128]{3,2,1,0:T(1,128)S(1)}, u32[]{:S(2)}, u32[]{:S(2)}) collective-permute-start(f32[4,6,1,128]{3,2,1,0:T(1,128)S(1)} %get-tuple-element.100), channel_id=1, source_target_pairs={{0,1},{1,2},{2,3},{4,5},{5,6},{6,7},{8,9},{9,10},{10,11},{12,13},{... | collective-permute-start | bytes 36872 | tf_op jit(solution)/shard_map/ppermute | solution.py:20
  396.9 7.7 %collective-permute-start.51 = (f32[4,6,1,128]{3,2,1,0:T(1,128)S(1)}, f32[4,6,1,128]{3,2,1,0:T(1,128)S(1)}, u32[]{:S(2)}, u32[]{:S(2)}) collective-permute-start(f32[4,6,1,128]{3,2,1,0:T(1,128)S(1)} %get-tuple-element.101), channel_id=1, source_target_pairs={{1,0},{2,1},{3,2},{5,4},{6,5},{7,6},{9,8},{10,9},{11,10},{13,12},{... | collective-permute-start | bytes 36872 | tf_op jit(solution)/shard_map/ppermute | solution.py:23
  404.9 6.1 %collective-permute-start.52 = (f32[4,1,32,128]{3,2,1,0:T(8,128)S(1)}, f32[4,1,32,128]{3,2,1,0:T(8,128)S(1)}, u32[]{:S(2)}, u32[]{:S(2)}) collective-permute-start(f32[4,1,32,128]{3,2,1,0:T(8,128)S(1)} %get-tuple-element.128), channel_id=1, source_target_pairs={{0,4},{4,8},{8,12},{12,16},{16,20},{20,24},{24,28},{28,32},{32,36}... | collective-permute-start | bytes 196616 | tf_op jit(solution)/shard_map/ppermute | solution.py:20
  409.7 3.9 collective-permute-start.53
  413.6 6.8 %collective-permute-start.54 = (f32[4,6,1,128]{3,2,1,0:T(1,128)S(1)}, f32[4,6,1,128]{3,2,1,0:T(1,128)S(1)}, u32[]{:S(2)}, u32[]{:S(2)}) collective-permute-start(f32[4,6,1,128]{3,2,1,0:T(1,128)S(1)} %get-tuple-element.98), channel_id=1, source_target_pairs={{0,1},{1,2},{2,3},{4,5},{5,6},{6,7},{8,9},{9,10},{10,11},{12,13},{... | collective-permute-start | bytes 36872 | tf_op jit(solution)/shard_map/ppermute | solution.py:20
  415.5 7.7 %collective-permute-start.55 = (f32[4,6,1,128]{3,2,1,0:T(1,128)S(1)}, f32[4,6,1,128]{3,2,1,0:T(1,128)S(1)}, u32[]{:S(2)}, u32[]{:S(2)}) collective-permute-start(f32[4,6,1,128]{3,2,1,0:T(1,128)S(1)} %get-tuple-element.99), channel_id=1, source_target_pairs={{1,0},{2,1},{3,2},{5,4},{6,5},{7,6},{9,8},{10,9},{11,10},{13,12},{... | collective-permute-start | bytes 36872 | tf_op jit(solution)/shard_map/ppermute | solution.py:23
  423.6 6.4 %collective-permute-start.56 = (f32[4,1,32,128]{3,2,1,0:T(8,128)S(1)}, f32[4,1,32,128]{3,2,1,0:T(8,128)S(1)}, u32[]{:S(2)}, u32[]{:S(2)}) collective-permute-start(f32[4,1,32,128]{3,2,1,0:T(8,128)S(1)} %get-tuple-element.126), channel_id=1, source_target_pairs={{0,4},{4,8},{8,12},{12,16},{16,20},{20,24},{24,28},{28,32},{32,36}... | collective-permute-start | bytes 196616 | tf_op jit(solution)/shard_map/ppermute | solution.py:20
  428.6 3.8 collective-permute-start.57
  432.4 6.8 %collective-permute-start.58 = (f32[4,6,1,128]{3,2,1,0:T(1,128)S(1)}, f32[4,6,1,128]{3,2,1,0:T(1,128)S(1)}, u32[]{:S(2)}, u32[]{:S(2)}) collective-permute-start(f32[4,6,1,128]{3,2,1,0:T(1,128)S(1)} %get-tuple-element.96), channel_id=1, source_target_pairs={{0,1},{1,2},{2,3},{4,5},{5,6},{6,7},{8,9},{9,10},{10,11},{12,13},{... | collective-permute-start | bytes 36872 | tf_op jit(solution)/shard_map/ppermute | solution.py:20
  434.3 7.7 %collective-permute-start.59 = (f32[4,6,1,128]{3,2,1,0:T(1,128)S(1)}, f32[4,6,1,128]{3,2,1,0:T(1,128)S(1)}, u32[]{:S(2)}, u32[]{:S(2)}) collective-permute-start(f32[4,6,1,128]{3,2,1,0:T(1,128)S(1)} %get-tuple-element.97), channel_id=1, source_target_pairs={{1,0},{2,1},{3,2},{5,4},{6,5},{7,6},{9,8},{10,9},{11,10},{13,12},{... | collective-permute-start | bytes 36872 | tf_op jit(solution)/shard_map/ppermute | solution.py:23
  442.5 6.2 %collective-permute-start.60 = (f32[8,1,32,128]{3,2,1,0:T(8,128)S(1)}, f32[8,1,32,128]{3,2,1,0:T(8,128)S(1)}, u32[]{:S(2)}, u32[]{:S(2)}) collective-permute-start(f32[8,1,32,128]{3,2,1,0:T(8,128)S(1)} %get-tuple-element.94), channel_id=1, source_target_pairs={{0,4},{4,8},{8,12},{12,16},{16,20},{20,24},{24,28},{28,32},{32,36}... | collective-permute-start | bytes 393224 | tf_op jit(solution)/shard_map/ppermute | solution.py:20
  447.4 3.9 collective-permute-start.61
  451.3 8.2 %collective-permute-start.62 = (f32[8,6,1,128]{3,2,1,0:T(1,128)S(1)}, f32[8,6,1,128]{3,2,1,0:T(1,128)S(1)}, u32[]{:S(2)}, u32[]{:S(2)}) collective-permute-start(f32[8,6,1,128]{3,2,1,0:T(1,128)S(1)} %get-tuple-element.86), channel_id=1, source_target_pairs={{0,1},{1,2},{2,3},{4,5},{5,6},{6,7},{8,9},{9,10},{10,11},{12,13},{... | collective-permute-start | bytes 73736 | tf_op jit(solution)/shard_map/ppermute | solution.py:20
  453.2 7.8 %collective-permute-start.63 = (f32[8,6,1,128]{3,2,1,0:T(1,128)S(1)}, f32[8,6,1,128]{3,2,1,0:T(1,128)S(1)}, u32[]{:S(2)}, u32[]{:S(2)}) collective-permute-start(f32[8,6,1,128]{3,2,1,0:T(1,128)S(1)} %get-tuple-element.87), channel_id=1, source_target_pairs={{1,0},{2,1},{3,2},{5,4},{6,5},{7,6},{9,8},{10,9},{11,10},{13,12},{... | collective-permute-start | bytes 73736 | tf_op jit(solution)/shard_map/ppermute | solution.py:23
  (24 other events, 376.4 us)
Sparse Core Ops, SparseCore 0:
  462.3 90.6 all-reduce.20
